TPU v7x, 32 devices: a whole 2x2x4 slice. The times are simulated.
32 devices in a mesh: elem: 8 (over z, x), lev: 4 (over y, core).
Axes of the slice: x: 2, y: 2, z: 4, core: 2. Of those that a mesh axis runs over, the one named last changes fastest.
Arguments:
- cloud_state: float32 [1024, 8, 4096], P(('elem', 'lev')), may hold values from -6 to 6
- substeps: int32 [1024], P('elem'), may hold values from 4 to 16
- element_links: int32 [256, 4], P('elem'), may hold values from 0 to 255, as said below
- host_state: float32 [4, 64, 4096], P(None, 'lev', 'elem'), may hold values from -6 to 6
- wind_field: float32 [2, 64, 4096], P(None, 'lev', 'elem'), may hold values from -3 to 3
- node_mass: float32 [4096], P('elem'), may hold values from 0.25 to 4
- field_coupling: float32 [8, 8], replicated, may hold values from -2 to 2
- force_map: float32 [8, 4], replicated, may hold values from -3 to 3
- feedback_map: float32 [4, 8], replicated, may hold values from -5 to 5
Outputs:
- cloud_new: float32 [1024, 8, 4096], P(('elem', 'lev'))
- host_new: float32 [4, 64, 4096], P(None, 'lev', 'elem')
Inputs may be any that keep to these rules, and one draw needn't show every extreme that they name: `element_links`: the 256 elements form a doubly periodic grid of 16 rows in which each index of elem holds two neighbouring grid columns, all rows, in some order; element e lies on index e // 32 of elem. Entries 0 to 3 of row e give the global index of the element to the left, right, below and above element e. An element's right edge meets its right neighbour's left edge node for node (same j), its upper edge its upper neighbour's lower edge (same i). The left neighbour lies on the same index of elem or the one before it (cyclically), the right one on the same or the one after it, the lower and upper ones on the same index.
All inputs are finite; a program needn't handle non-finite values.
Results may differ from a plain program's by a relative error of at most 0.0003.
Values sent between devices are 32-bit elements; how exact they have to be, the bound alone decides.
A program may use at most 128 MiB of HBM per device.

v0:
```python
import jax
import jax.numpy as jnp
import numpy as np
from jax import lax
from jax.sharding import PartitionSpec as P

CRM_X = 64


lateral_mix = 0.2
vertical_mix = 0.2
cloud_step = 0.1
host_step = 0.1
host_mix = 0.2
highest = lax.Precision.HIGHEST


def padded_2(cells, sides, width, closed):
    for axis, dim in sides:
        count = lax.axis_size(axis)
        ends = count if closed else count - 1
        head = lax.slice_in_dim(cells, 0, width, axis=dim)
        tail = lax.slice_in_dim(cells, cells.shape[dim] - width, cells.shape[dim], axis=dim)
        cells = jnp.concatenate(
            [
                lax.ppermute(tail, axis, [(i, (i + 1) % count) for i in range(ends)]),
                cells,
                lax.ppermute(head, axis, [((i + 1) % count, i) for i in range(ends)]),
            ],
            axis=dim,
        )
    return cells


def gll_derivative():
    points = np.array([-1.0, -1.0 / np.sqrt(5.0), 1.0 / np.sqrt(5.0), 1.0])
    weights = np.array(
        [
            1.0 / np.prod([points[index] - points[other] for other in range(4) if other != index])
            for index in range(4)
        ]
    )
    matrix = np.zeros((4, 4))
    for target in range(4):
        for source in range(4):
            if target != source:
                matrix[target, source] = (
                    weights[source] / weights[target] / (points[target] - points[source])
                )
        matrix[target, target] = -np.sum(matrix[target])
    return matrix


def advance_clouds(cloud, driving, counts, coupling):
    n_rows, n_fields, n_cells = cloud.shape
    cell_width = CRM_X
    n_levels = n_cells // cell_width
    spread = jnp.repeat(driving, cell_width, axis=2)

    def one_step(stepno, current):
        extended = jnp.pad(current, ((0, 0), (0, 0), (cell_width, cell_width)))
        upper_cells = extended[:, :, 2 * cell_width :]
        lower_cells = extended[:, :, : -2 * cell_width]
        shaped = current.reshape(n_rows, n_fields, n_levels, cell_width)
        eastward = jnp.roll(shaped, -1, axis=3).reshape(current.shape)
        westward = jnp.roll(shaped, 1, axis=3).reshape(current.shape)
        reaction = jnp.tanh(jnp.einsum("gf,nfc->ngc", coupling, current, precision=highest))
        update = (
            current
            + (
                lateral_mix * (eastward + westward - 2.0 * current)
                + vertical_mix * (upper_cells + lower_cells - 2.0 * current)
            )
            + cloud_step * (reaction + spread)
        )
        return jnp.where((stepno < counts)[:, None, None], update, current)

    return lax.fori_loop(0, jnp.max(counts), one_step, cloud)


def edge_tables(element_links, n_nodes):
    elem_dev = n_nodes // 16
    quarter = 4 * elem_dev
    my_index = lax.axis_index("elem")
    node_ids = jnp.arange(n_nodes, dtype=jnp.int32)
    elem_of = node_ids // 16
    row_of = node_ids // 4 % 4
    col_of = node_ids % 4
    edge_ids = jnp.arange(2 * quarter, dtype=jnp.int32)
    inner = edge_ids % quarter
    edge_node = inner // 4 * 16 + inner % 4 * 4 + jnp.where(edge_ids < quarter, 0, 3)
    picker = (node_ids[:, None] == edge_node[None, :]).astype(jnp.float32)
    left_ids = element_links[:, 0][elem_of]
    right_ids = element_links[:, 1][elem_of]
    left_base = jnp.where(left_ids // elem_dev == my_index, 2 * quarter, 0)
    right_base = jnp.where(right_ids // elem_dev == my_index, 2 * quarter, 4 * quarter)
    left_source = left_base + quarter + left_ids % elem_dev * 4 + row_of
    right_source = right_base + right_ids % elem_dev * 4 + row_of
    side_source = jnp.where(col_of == 0, left_source, jnp.where(col_of == 3, right_source, -1))
    sideways = (jnp.arange(6 * quarter, dtype=jnp.int32)[:, None] == side_source[None, :]).astype(
        jnp.float32
    )
    lower_ids = element_links[:, 2][elem_of] % elem_dev
    upper_ids = element_links[:, 3][elem_of] % elem_dev
    lower_source = lower_ids * 16 + 12 + col_of
    upper_source = upper_ids * 16 + col_of
    vert_source = jnp.where(row_of == 0, lower_source, jnp.where(row_of == 3, upper_source, -1))
    vertical = (node_ids[:, None] == vert_source[None, :]).astype(jnp.float32)
    return (picker, sideways, vertical)


def edge_sum(quantity, tables):
    picker, sideways, vertical = tables
    lead, levels, n_nodes = quantity.shape
    flat = quantity.reshape(lead * levels, n_nodes)
    edges = jnp.dot(flat, picker, precision=highest).reshape(lead, levels, picker.shape[1])
    with_peers = padded_2(edges, (("elem", 2),), picker.shape[1], True)
    first = flat + jnp.dot(
        with_peers.reshape(lead * levels, sideways.shape[0]), sideways, precision=highest
    )
    second = first + jnp.dot(first, vertical, precision=highest)
    return second.reshape(lead, levels, n_nodes)


def shards(
    cloud_state,
    substeps,
    element_links,
    host_state,
    wind_field,
    node_mass,
    field_coupling,
    force_map,
    feedback_map,
):
    own_rows, n_fields, n_cells = cloud_state.shape
    n_vars, lev_dev, n_nodes = host_state.shape
    n_cols = substeps.shape[0]
    elem_dev = n_nodes // 16
    cell_width = CRM_X
    lev_count = lax.axis_size("lev")
    lev_at = lax.axis_index("lev")
    node_ids = jnp.arange(n_nodes)
    column_of_node = node_ids // 16 * 4 + node_ids // 4 % 4 // 2 * 2 + node_ids % 4 // 2
    member = (column_of_node[:, None] == jnp.arange(n_cols)[None, :]).astype(jnp.float32)
    pooling = 0.25 * member
    host_flat = host_state.reshape(n_vars * lev_dev, n_nodes)
    host_columns = (
        jnp.dot(host_flat, pooling, precision=highest)
        .reshape(n_vars, lev_dev, n_cols)
        .transpose(2, 0, 1)
    )
    whole_host = lax.all_to_all(
        host_columns.reshape(lev_count, own_rows, n_vars, lev_dev),
        "lev",
        split_axis=0,
        concat_axis=3,
        tiled=True,
    ).reshape(own_rows, n_vars, lev_dev * lev_count)
    driving = jnp.einsum("fv,nvl->nfl", force_map, whole_host, precision=highest)
    own_counts = lax.dynamic_slice_in_dim(substeps, lev_at * own_rows, own_rows, 0)
    cloud_new = advance_clouds(cloud_state, driving, own_counts, field_coupling)
    n_levels = n_cells // cell_width
    change = (
        (cloud_new - cloud_state).reshape(own_rows, n_fields, n_levels, cell_width).mean(axis=3)
    )
    level_change = lax.all_to_all(
        change.reshape(1, own_rows, n_fields, n_levels),
        "lev",
        split_axis=3,
        concat_axis=0,
        tiled=True,
    ).reshape(n_cols, n_fields, lev_dev)
    column_tendency = jnp.einsum("vf,nfl->vln", feedback_map, level_change, precision=highest)
    physics = jnp.dot(
        column_tendency.reshape(n_vars * lev_dev, n_cols), member.T, precision=highest
    ).reshape(n_vars, lev_dev, n_nodes)
    derivative = gll_derivative()
    kron_x = jnp.asarray(np.kron(np.eye(elem_dev * 4), derivative).T, jnp.float32)
    kron_y = jnp.asarray(np.kron(np.eye(elem_dev), np.kron(derivative, np.eye(4))).T, jnp.float32)

    def tendency(field):
        flat = field.reshape(n_vars * lev_dev, n_nodes)
        along_x = jnp.dot(flat, kron_x, precision=highest).reshape(field.shape)
        along_y = jnp.dot(flat, kron_y, precision=highest).reshape(field.shape)
        padded = padded_2(field, (("lev", 1),), 1, False)
        return (
            -(wind_field[0] * along_x + wind_field[1] * along_y)
            + host_mix * (padded[:, 2:] + padded[:, :-2] - 2.0 * field)
            + physics
        )

    tables = edge_tables(element_links, n_nodes)
    mass_total = edge_sum(node_mass.reshape(1, 1, n_nodes), tables)

    def smooth(values):
        return edge_sum(node_mass * values, tables) / mass_total

    first_section = smooth(host_state + host_step * tendency(host_state))
    second_section = smooth(
        0.75 * host_state + 0.25 * (first_section + host_step * tendency(first_section))
    )
    host_new = smooth(
        host_state / 3.0 + 2.0 / 3.0 * (second_section + host_step * tendency(second_section))
    )
    return (cloud_new, host_new)


def solution(mesh):
    placed = (
        P(("elem", "lev"), None, None),
        P("elem"),
        P("elem", None),
        P(None, "lev", "elem"),
        P(None, "lev", "elem"),
        P("elem"),
        P(),
        P(),
        P(),
    )
    return jax.shard_map(
        shards,
        mesh=mesh,
        in_specs=placed,
        out_specs=(P(("elem", "lev"), None, None), P(None, "lev", "elem")),
        check_vma=False,
    )
```

profile of v0, /device:TPU:0, one launch (start us, length us, event | category | flops | bytes accessed | tf_op | source)
XLA Modules:
  0.0 1451.9 jit_solution(4457423744663804279)
XLA Ops:
  52.5 4.5 select_select_fusion
  57.0 32.0 %fusion.110 = s32[512]{0:T(512)} fusion(pred[512]{0:T(512)(128)(4,1)S(1)} %compare_reduce_fusion, pred[512]{0:T(512)(128)(4,1)S(1)} %compare_reduce_fusion.1, pred[512]{0:T(512)(128)(4,1)S(1)} %compare_reduce_fusion.2, pred[512]{0:T(512)(128)(4,1)S(1)} %compare_reduce_fusion.3, pred[512]{0:T(512)(128)(4,1)S(1)} %compare_reduce_fusion.4, ...), kind=kLoop, calls=%fused_computation.207 | loop fusion | flops 53248 | bytes 19144 | tf_op jit(solution)/shard_map/jit(_where)/select_n | solution.py:107
  89.0 31.8 %fusion.100 = s32[512]{0:T(512)} fusion(pred[512]{0:T(512)(128)(4,1)S(1)} %compare_reduce_fusion, pred[512]{0:T(512)(128)(4,1)S(1)} %compare_reduce_fusion.1, pred[512]{0:T(512)(128)(4,1)S(1)} %compare_reduce_fusion.2, pred[512]{0:T(512)(128)(4,1)S(1)} %compare_reduce_fusion.3, pred[512]{0:T(512)(128)(4,1)S(1)} %compare_reduce_fusion.4, ...), kind=kLoop, calls=%fused_computation.197 | loop fusion | flops 64512 | bytes 19148 | tf_op jit(solution)/shard_map/jit(_where)/select_n | solution.py:99
  122.1 4.7 copy.36
  128.5 471.9 %while.13 = (s32[]{:T(128)}, f32[32,8,4096]{2,1,0:T(8,128)}, s32[]{:T(128)}, s32[32]{0:T(128)S(1)}, f32[8,8]{1,0:T(8,128)S(1)}, /*index=5*/f32[32,8,64]{2,1,0:T(8,128)S(1)}, s32[]{:T(128)}) while((s32[]{:T(128)}, f32[32,8,4096]{2,1,0:T(8,128)}, s32[]{:T(128)}, s32[32]{0:T(128)S(1)}, f32[8,8]{1,0:T(8,128)S(1)}, ...), condition=%wide.region_2.3_spmd.clone, body=%wide.region_1.2_spmd.clone.sunk | while | flops 115343392 | bytes 104923696 | solution.py:78
  129.3 4.7 copy.44
  134.0 7.9 reshape.1027
  141.9 11.1 fusion.180
  153.0 7.1 fusion.181
  160.2 13.2 maximum_add_fusion.2
  173.4 7.9 add.913
  181.3 4.5 broadcast_in_dim.62
  185.8 7.9 reshape.1026
  193.7 13.5 fusion.182
  207.8 4.7 copy.44
  212.5 7.9 reshape.1027
  220.4 11.1 fusion.180
  231.5 7.1 fusion.181
  238.6 13.2 maximum_add_fusion.2
  251.9 7.9 add.913
  259.8 4.5 broadcast_in_dim.62
  264.3 7.9 reshape.1026
  272.2 13.5 fusion.182
  286.3 4.7 copy.44
  291.0 7.9 reshape.1027
  298.8 11.1 fusion.180
  310.0 7.1 fusion.181
  317.1 13.2 maximum_add_fusion.2
  330.3 7.9 add.913
  338.2 4.5 broadcast_in_dim.62
  342.8 7.9 reshape.1026
  350.7 13.5 fusion.182
  364.8 4.7 copy.44
  369.5 7.9 reshape.1027
  377.3 11.1 fusion.180
  388.5 7.1 fusion.181
  395.6 13.2 maximum_add_fusion.2
  408.8 7.9 add.913
  416.7 4.5 broadcast_in_dim.62
  421.2 7.9 reshape.1026
  429.1 13.5 fusion.182
  443.2 4.7 copy.44
  447.9 7.9 reshape.1027
  455.8 11.1 fusion.180
  466.9 7.1 fusion.181
  474.0 13.2 maximum_add_fusion.2
  487.3 7.9 add.913
  495.2 4.5 broadcast_in_dim.62
  499.7 7.9 reshape.1026
  507.6 13.5 fusion.182
  521.7 4.7 copy.44
  526.4 7.9 reshape.1027
  534.3 11.1 fusion.180
  545.4 7.1 fusion.181
  552.5 13.2 maximum_add_fusion.2
  565.8 7.9 add.913
  573.7 4.5 broadcast_in_dim.62
  578.2 7.9 reshape.1026
  586.1 13.5 fusion.182
  600.4 6.1 sub.95
  606.5 7.9 reshape.426
  614.4 5.7 reduce_sum.9
  632.3 4.7 collective-permute-start.3
  646.8 782.1 %collective-permute-start.8 = (f32[4,16,256]{2,1,0:T(8,128)S(1)}, f32[4,16,256]{2,1,0:T(8,128)S(1)}, u32[]{:S(2)}, u32[]{:S(2)}) collective-permute-start(f32[4,16,256]{2,1,0:T(8,128)S(1)} %fusion.35), channel_id=1, source_target_pairs={{0,4},{4,8},{8,12},{12,16},{16,20},{20,24},{24,28},{28,0},{1,5},{5... | collective-permute-start | bytes 196616 | tf_op jit(solution)/shard_map/ppermute | solution.py:26
  (173 shorter events, 99.4 us)
Async XLA Ops:
  0.6 127.5 %copy-start = (f32[8,4]{0,1:T(4,128)S(1)}, f32[8,4]{0,1:T(4,128)}, u32[]{:S(2)}) copy-start(f32[8,4]{0,1:T(4,128)} %param.20) | copy-start | bytes 388
  0.7 8.8 copy-start.12
  2.2 622.3 %collective-permute-start.4 = (f32[1,1,256]{2,1,0:T(1,128)}, f32[1,1,256]{2,1,0:T(1,128)}, u32[]{:S(2)}, u32[]{:S(2)}) collective-permute-start(f32[1,1,256]{2,1,0:T(1,128)} %convolution_bitcast_fusion.4), channel_id=1, source_target_pairs={{0,4},{4,8},{8,12},{12,16},{16,20},{20,24},{24,28},{28,0},{1,5},{5... | collective-permute-start | bytes 3080 | tf_op jit(solution)/shard_map/ppermute | solution.py:26
  5.1 619.3 %collective-permute-start.5 = (f32[1,1,256]{2,1,0:T(1,128)}, f32[1,1,256]{2,1,0:T(1,128)}, u32[]{:S(2)}, u32[]{:S(2)}) collective-permute-start(f32[1,1,256]{2,1,0:T(1,128)} %convolution_bitcast_fusion.4), channel_id=1, source_target_pairs={{4,0},{8,4},{12,8},{16,12},{20,16},{24,20},{28,24},{0,28},{5,1},{9... | collective-permute-start | bytes 3080 | tf_op jit(solution)/shard_map/ppermute | solution.py:28
  8.2 1.3 copy-start.14
  10.4 116.4 %all-to-all-start = ((f32[4,1,2048]{2,1,0:T(1,128)}), f32[4,1,2048]{2,1,0:T(1,128)S(1)}, u32[]{:S(2)}, u32[]{:S(2)}) async-start(f32[4,1,2048]{2,1,0:T(1,128)} %reshape.1020), calls=%async_computation | async-start | bytes 65536 | tf_op jit(solution)/shard_map/all_to_all | solution.py:153
  15.1 615.2 %collective-permute-start = (f32[4,1,512]{2,1,0:T(1,128)}, f32[4,1,512]{2,1,0:T(1,128)}, u32[]{:S(2)}, u32[]{:S(2)}) collective-permute-start(f32[4,1,512]{2,1,0:T(1,128)} %get-tuple-element.121), channel_id=1, source_target_pairs={{1,0},{2,1},{3,2},{5,4},{6,5},{7,6},{9,8},{10,9},{11,10},{13,12},{... | collective-permute-start | bytes 24584 | tf_op jit(solution)/shard_map/ppermute | solution.py:28
  16.4 613.9 %collective-permute-start.1 = (f32[4,1,512]{2,1,0:T(1,128)}, f32[4,1,512]{2,1,0:T(1,128)}, u32[]{:S(2)}, u32[]{:S(2)}) collective-permute-start(f32[4,1,512]{2,1,0:T(1,128)} %get-tuple-element.122), channel_id=1, source_target_pairs={{0,1},{1,2},{2,3},{4,5},{5,6},{6,7},{8,9},{9,10},{10,11},{12,13},{... | collective-permute-start | bytes 24584 | tf_op jit(solution)/shard_map/ppermute | solution.py:26
  36.8 90.0 %copy-start.8 = (f32[16,512]{1,0:T(8,128)}, f32[16,512]{1,0:T(8,128)S(1)}, u32[]{:S(2)}) copy-start(f32[16,512]{1,0:T(8,128)S(1)} %get-tuple-element.124) | copy-start | bytes 98308
  122.1 6.4 copy-start.10
  141.9 11.1 copy-start.2
  220.4 11.1 copy-start.2
  298.8 11.1 copy-start.2
  377.3 11.1 copy-start.2
  455.8 11.1 copy-start.2
  534.3 11.1 copy-start.2
  614.4 10.1 copy-start.18
  614.4 11.4 copy-start.11
  614.4 15.4 %copy-start.16 = (f32[4,8]{1,0:T(4,128)S(1)}, f32[4,8]{1,0:T(4,128)}, u32[]{:S(2)}) copy-start(f32[4,8]{1,0:T(4,128)} %param.21) | copy-start | bytes 388
  614.4 15.6 %copy-start.15 = (s32[512]{0:T(512)S(1)}, s32[512]{0:T(512)}, u32[]{:S(2)}) copy-start(s32[512]{0:T(512)} %copy-done.14) | copy-start | bytes 6148
  614.4 16.0 %copy-start.3 = (f32[512,512,1]{1,0,2:T(8,128)S(1)}, f32[512,512,1]{1,0,2:T(8,128)}, u32[]{:S(2)}) copy-start(f32[512,512,1]{1,0,2:T(8,128)} %constant.371) | copy-start | bytes 3145732
  614.4 16.0 %copy-start.5 = (f32[4,16,512]{2,1,0:T(8,128)S(1)}, f32[4,16,512]{2,1,0:T(8,128)}, u32[]{:S(2)}) copy-start(f32[4,16,512]{2,1,0:T(8,128)} %param.16) | copy-start | bytes 393220
  614.4 16.0 %copy-start.6 = (f32[16,512]{1,0:T(8,128)S(1)}, f32[16,512]{1,0:T(8,128)}, u32[]{:S(2)}) copy-start(f32[16,512]{1,0:T(8,128)} %get-tuple-element.123) | copy-start | bytes 98308
  614.4 16.0 %copy-start.7 = (f32[4,16,512]{2,1,0:T(8,128)S(1)}, f32[4,16,512]{2,1,0:T(8,128)}, u32[]{:S(2)}) copy-start(f32[4,16,512]{2,1,0:T(8,128)} %fusion.12) | copy-start | bytes 393220
  620.2 11.8 copy-start.13
  620.2 16.9 %copy-start.17 = (s32[512]{0:T(512)S(1)}, s32[512]{0:T(512)}, u32[]{:S(2)}) copy-start(s32[512]{0:T(512)} %fusion.110) | copy-start | bytes 6148
  620.2 24.7 %copy-start.4 = (f32[512,512,1]{1,0,2:T(8,128)S(1)}, f32[512,512,1]{1,0,2:T(8,128)}, u32[]{:S(2)}) copy-start(f32[512,512,1]{1,0,2:T(8,128)} %constant.372) | copy-start | bytes 3145732
  620.2 24.7 %copy-start.9 = (f32[16,512]{1,0:T(8,128)S(1)}, f32[16,512]{1,0:T(8,128)}, u32[]{:S(2)}) copy-start(f32[16,512]{1,0:T(8,128)} %copy-done.8) | copy-start | bytes 98308
  621.2 7.4 all-to-all-start.1
  632.3 7.0 collective-permute-start.2
  632.3 7.0 collective-permute-start.3
  640.5 5.1 collective-permute-start.6
  641.8 3.8 collective-permute-start.7
  644.9 807.0 %copy-start.1 = (f32[8,4]{0,1:T(4,128)S(1)}, f32[8,4]{0,1:T(4,128)}, u32[]{:S(2)}) copy-start(f32[8,4]{0,1:T(4,128)} %param.20) | copy-start | bytes 388
  646.8 784.0 %collective-permute-start.8 = (f32[4,16,256]{2,1,0:T(8,128)S(1)}, f32[4,16,256]{2,1,0:T(8,128)S(1)}, u32[]{:S(2)}, u32[]{:S(2)}) collective-permute-start(f32[4,16,256]{2,1,0:T(8,128)S(1)} %fusion.35), channel_id=1, source_target_pairs={{0,4},{4,8},{8,12},{12,16},{16,20},{20,24},{24,28},{28,0},{1,5},{5... | collective-permute-start | bytes 196616 | tf_op jit(solution)/shard_map/ppermute | solution.py:26
  1428.9 4.3 collective-permute-start.9
  1434.5 5.4 collective-permute-start.10
  1435.8 4.1 collective-permute-start.11
  1441.0 7.1 collective-permute-start.12
  1443.9 6.2 collective-permute-start.13
where the time goes:
time: 1460 us; the launch traced here: 1450 us
  starting transfers between devices  818 us (56%)
  local copies, waits for them, and re-layouts  340 us (23%)
  other arithmetic  177 us (12%)
  matrix products  97.9 us (7%)
    ppermute x7, starting transfers between devices, padded_2(): lax.ppermute(tail, axis, [(i, (i + 1) % count) for i in range(ends)])  798 us
    slice x12, local copies, waits for them, and re-layouts, one_step(): westward = jnp.roll(shaped, 1, axis=3).reshape(current.shape)  110 us
    dot_general x6, matrix products, one_step(): jnp.einsum('gf,nfc->ngc', coupling, current, precision=highest)  80.8 us
    add x6, other arithmetic, one_step(): eastward + westward - 2.0 * current  79.4 us
    add x6, local copies, waits for them, and re-layouts, one_step(): eastward + westward - 2.0 * current  47.4 us
    reshape x6, local copies, waits for them, and re-layouts, advance_clouds(): spread = jnp.repeat(driving, cell_width, axis=2)  47.3 us
    reshape x6, local copies, waits for them, and re-layouts, one_step(): shaped = current.reshape(n_rows, n_fields, n_levels, cell_width)  47.1 us
    select_n x1, other arithmetic, edge_tables(): jnp.where(row_of == 0, lower_source, jnp.where(row_of == 3, upper_source,...  32 us
  transfers between devices with their start and end apart: 16, of which 6 were waited for; matrix products, arithmetic and copies ran while one was open for 42% of the time, Pallas kernels for 0%

commit v1 on v0

v1 whole, which is shorter than its diff:
```python
import functools

import jax
import jax.numpy as jnp
import ml_dtypes
import numpy as np
from jax import lax
from jax.experimental import pallas as pl
from jax.experimental.pallas import tpu as pltpu
from jax.sharding import PartitionSpec as P

CRM_X = 64
HALO = 4
LANES = 128
PAIR = 256

mix = 0.2
cloud_step = 0.1
host_step = 0.1
host_mix = 0.2
bf16 = jnp.bfloat16
f32 = jnp.float32
highest = lax.Precision.HIGHEST
vmem = pl.BlockSpec(memory_space=pltpu.VMEM)
smem = pl.BlockSpec(memory_space=pltpu.SMEM)
params = pltpu.CompilerParams(vmem_limit_bytes=48 * 1024 * 1024)


def gll_derivative():
    points = np.array([-1.0, -1.0 / np.sqrt(5.0), 1.0 / np.sqrt(5.0), 1.0])
    weights = np.array(
        [
            1.0 / np.prod([points[index] - points[other] for other in range(4) if other != index])
            for index in range(4)
        ]
    )
    matrix = np.zeros((4, 4))
    for target in range(4):
        for source in range(4):
            if target != source:
                matrix[target, source] = (
                    weights[source] / weights[target] / (points[target] - points[source])
                )
        matrix[target, target] = -np.sum(matrix[target])
    return matrix


def split(x):
    hi = x.astype(bf16)
    return hi, (x - hi.astype(f32)).astype(bf16)


def mm(a, b):
    return jnp.dot(a, b, preferred_element_type=f32)


def dot_exact_right(x, b):
    hi, lo = split(x)
    return mm(hi, b) + mm(lo, b)


def dot3(a, b):
    a_hi, a_lo = split(a)
    b_hi, b_lo = split(b)
    return mm(a_hi, b_hi) + mm(a_hi, b_lo) + mm(a_lo, b_hi)


def iota(shape, dim):
    return lax.broadcasted_iota(jnp.int32, shape, dim)


def one_hot(cond):
    return jnp.where(cond, 1.0, 0.0).astype(bf16)


def cloud_kernel(
    ends, row_counts, cells, kron, force, feed, columns, out, tend,
    state, spread, k_wide, k_low, parts, change,
):
    rows, n_cells = cells.shape
    half = n_cells // 2
    levels = n_cells // CRM_X
    blocks = half // LANES
    group = 32

    k_hi, k_lo = split(kron[...])
    k_wide[:, :rows] = k_hi
    k_wide[:, rows:] = k_hi
    k_low[...] = k_lo
    driving = cloud_step * dot3(force[...], columns[...])
    src, dst = iota((PAIR, PAIR), 0), iota((PAIR, PAIR), 1)
    weave = one_hot(src == dst % 2 * LANES + dst // LANES * CRM_X + dst % LANES // 2)
    unweave = one_hot(dst == src % 2 * LANES + src // LANES * CRM_X + src % LANES // 2)
    odd = iota((rows, LANES), 1) % 2 == 1

    def ends_of(slot):
        last = state[slot, :, pl.ds(half * 2, LANES)]
        first = state[slot, :, pl.ds(LANES, LANES)]
        state[slot, :, pl.ds(0, LANES)] = jnp.where(odd, pltpu.roll(last, 1, 1), 0.0)
        state[slot, :, pl.ds(half * 2 + LANES, LANES)] = jnp.where(
            odd, 0.0, pltpu.roll(first, LANES - 1, 1)
        )

    def pair_of(ref, k):
        near = pl.multiple_of(k * LANES, LANES)
        far = pl.multiple_of(half + k * LANES, LANES)
        return jnp.concatenate([ref[:, pl.ds(near, LANES)], ref[:, pl.ds(far, LANES)]], axis=1)

    def enter(k, carry):
        at = pl.multiple_of(k * PAIR, LANES)
        state[0, :, pl.ds(pl.multiple_of(at + LANES, LANES), PAIR)] = dot_exact_right(
            pair_of(cells, k), weave
        )
        lane = iota((levels, PAIR), 1)
        level = 2 * k + lane // LANES + lane % 2 * (levels // 2)
        spread[:, pl.ds(at, PAIR)] = dot_exact_right(
            driving, one_hot(iota((levels, PAIR), 0) == level)
        )
        return carry

    lax.fori_loop(0, blocks, enter, 0)
    ends_of(0)

    def step_of(masked):
        def step(s, carry):
            now = s % 2
            later = 1 - now

            def block(k, inner):
                at = pl.multiple_of(k * PAIR, LANES)
                mid = pl.multiple_of(at + LANES, LANES)
                for g in range(0, rows, group):
                    hi, lo = split(state[now, pl.ds(g, group), pl.ds(mid, PAIR)])
                    parts[pl.ds(g, group), :] = hi
                    parts[pl.ds(rows + g, group), :] = lo
                react = mm(k_wide[...], parts[...]) + mm(k_low[...], parts[pl.ds(0, rows), :])
                for g in range(0, rows, group):
                    for c in range(0, PAIR, LANES):
                        take = lambda start: state[
                            now, pl.ds(g, group), pl.ds(pl.multiple_of(start, LANES), LANES)
                        ]
                        x = take(mid + c)
                        total = (x + (take(at + c) + take(mid + c + LANES))) + (
                            pltpu.roll(x, 2, 1) + pltpu.roll(x, LANES - 2, 1)
                        )
                        drive = spread[pl.ds(g, group), pl.ds(pl.multiple_of(at + c, LANES), LANES)]
                        new = mix * total + (
                            cloud_step * jnp.tanh(react[g : g + group, c : c + LANES]) + drive
                        )
                        if masked:
                            new = jnp.where(s < row_counts[pl.ds(g, group), :], new, x)
                        state[
                            later, pl.ds(g, group), pl.ds(pl.multiple_of(mid + c, LANES), LANES)
                        ] = new
                return inner

            lax.fori_loop(0, blocks, block, 0)
            ends_of(later)
            return carry

        return step

    lax.fori_loop(0, ends[0], step_of(False), 0)
    lax.fori_loop(ends[0], ends[1], step_of(True), 0)
    final = ends[1] % 2
    change[...] = jnp.zeros_like(change)

    def leave(k, carry):
        at = pl.multiple_of(k * PAIR + LANES, LANES)
        new = dot_exact_right(state[final, :, pl.ds(at, PAIR)], unweave)
        delta = new - pair_of(cells, k)
        out[:, pl.ds(pl.multiple_of(k * LANES, LANES), LANES)] = new[:, :LANES]
        out[:, pl.ds(pl.multiple_of(half + k * LANES, LANES), LANES)] = new[:, LANES:]
        lane = iota((PAIR, levels), 0)
        level = 2 * k + lane % LANES // CRM_X + lane // LANES * (levels // 2)
        mean = jnp.where(iota((PAIR, levels), 1) == level, 1.0 / CRM_X, 0.0).astype(bf16)
        change[...] += dot_exact_right(delta, mean)
        return carry

    lax.fori_loop(0, blocks, leave, 0)
    tend[...] = dot3(feed[...], change[...])


def spread_diagonal(matrix, count):
    height, width = matrix.shape
    tiled = jnp.tile(matrix, (count, count))
    row = iota(tiled.shape, 0) // height
    col = iota(tiled.shape, 1) // width
    return jnp.where(row == col, tiled, 0.0)


def run_clouds(cloud_state, columns, counts, coupling, force_map, feedback_map):
    own, n_fields, n_cells = cloud_state.shape
    n_vars = columns.shape[1]
    levels = n_cells // CRM_X
    rows = own * n_fields
    ends = jnp.stack([jnp.min(counts), jnp.max(counts)])
    row_counts = jnp.broadcast_to(counts[:, None, None], (own, n_fields, LANES))
    out, tend = pl.pallas_call(
        cloud_kernel,
        out_shape=(
            jax.ShapeDtypeStruct((rows, n_cells), f32),
            jax.ShapeDtypeStruct((own * n_vars, levels), f32),
        ),
        in_specs=[smem] + [vmem] * 6,
        out_specs=(vmem, vmem),
        scratch_shapes=[
            pltpu.VMEM((2, rows, n_cells + 2 * LANES), f32),
            pltpu.VMEM((rows, n_cells), f32),
            pltpu.VMEM((rows, 2 * rows), bf16),
            pltpu.VMEM((rows, rows), bf16),
            pltpu.VMEM((2 * rows, PAIR), bf16),
            pltpu.VMEM((rows, levels), f32),
        ],
        compiler_params=params,
        cost_estimate=pl.CostEstimate(
            flops=2 * 16 * 3 * rows * rows * n_cells,
            bytes_accessed=8 * rows * n_cells,
            transcendentals=16 * rows * n_cells,
        ),
        name="clouds",
    )(
        ends,
        row_counts.reshape(rows, LANES),
        cloud_state.reshape(rows, n_cells),
        spread_diagonal(coupling, own),
        spread_diagonal(force_map, own),
        spread_diagonal(feedback_map, own),
        columns.reshape(own * n_vars, levels),
    )
    return out.reshape(cloud_state.shape), tend.reshape(own, n_vars, levels)


def tables_kernel(sources, masses, gather, remote, inverse, *, elem_dev):
    n = gather.shape[0]
    edge = remote.shape[0] // 2
    node_r, node_c = iota((n, n), 0), iota((n, n), 1)
    own, left, right, vert = (sources[k : k + 1, :] for k in range(4))
    turn = one_hot((node_r == vert) | (node_r == node_c))
    local = one_hot((node_r == own) | (node_r == node_c))
    gather[...] = mm(local, turn).astype(bf16)
    at = iota((edge, n), 0)
    far = jnp.concatenate([one_hot(at == left), one_hot(at == right)], axis=0)
    remote[...] = mm(far, turn).astype(bf16)
    mass = masses[...]
    total = (
        dot_exact_right(mass, gather[...])
        + pltpu.roll(
            dot_exact_right(dot_exact_right(mass, picker(n, 3)), remote[pl.ds(0, edge), :]), 7, 0
        )
        + pltpu.roll(
            dot_exact_right(dot_exact_right(mass, picker(n, 0)), remote[pl.ds(edge, edge), :]), 6, 0
        )
    )
    inverse[...] = jnp.broadcast_to(1.0 / total[:1, :], inverse.shape)


def picker(n, side):
    node, at = iota((n, n // 4), 0), iota((n, n // 4), 1)
    return one_hot(node == at * 4 + side)


def advance(h0, h, wind_x, wind_y, physics, mass, derive, keep, take):
    rows, n = h.shape
    d_hi, d_lo = derive[pl.ds(0, LANES), :], derive[pl.ds(LANES, LANES), :]
    hi, lo = split(h)
    along = []
    for c in range(0, n, LANES):
        a, b = hi[:, c : c + LANES], lo[:, c : c + LANES]
        along.append(mm(a, d_hi) + mm(b, d_hi) + mm(a, d_lo))
    along_x = jnp.concatenate([a[:, :LANES] for a in along], axis=1)
    along_y = jnp.concatenate([a[:, LANES:] for a in along], axis=1)
    tendency = (
        host_mix * (pltpu.roll(h, 1, 0) + pltpu.roll(h, rows - 1, 0) - 2.0 * h)
        - (wind_x * along_x + wind_y * along_y)
        + physics
    )
    value = take * (h + host_step * tendency)
    if keep:
        value = value + keep * h0
    return mass * value


def send_edges(q, to_right, to_left):
    hi, lo = split(q)
    n = q.shape[1]
    right, left = picker(n, 3), picker(n, 0)
    to_right[...] = mm(hi, right) + mm(lo, right)
    to_left[...] = mm(hi, left) + mm(lo, left)


def first_kernel(h0, wind, column, mass, derive, q, to_right, to_left, physics):
    rows, n = h0.shape
    n_cols = column.shape[1]
    node = iota((n_cols, n), 1)
    home = node // 16 * 4 + node // 4 % 4 // 2 * 2 + node % 4 // 2
    physics[...] = dot_exact_right(column[...], one_hot(iota((n_cols, n), 0) == home))
    h = h0[...]
    value = advance(
        h, h, wind[0], wind[1], physics[...], mass[:1, :], derive, 0.0, 1.0
    )
    q[...] = value
    send_edges(value, to_right, to_left)


def joined(q, from_left, from_right, gather, remote, inverse, inside):
    edge = from_left.shape[1]
    total = (
        dot_exact_right(q[...], gather[...])
        + dot_exact_right(from_left[...], remote[pl.ds(0, edge), :])
        + dot_exact_right(from_right[...], remote[pl.ds(edge, edge), :])
    )
    return jnp.where(inside[:, :1] > 0.0, total * inverse[:1, :], 0.0)


def middle_kernel(
    q_in, from_left, from_right, gather, remote, inverse, inside,
    h0, wind, physics, mass, derive, q, to_right, to_left, *, keep, take,
):
    h = joined(q_in, from_left, from_right, gather, remote, inverse, inside)
    value = advance(
        h0[...], h, wind[0], wind[1], physics[...], mass[:1, :], derive, keep, take
    )
    q[...] = value
    send_edges(value, to_right, to_left)


def last_kernel(q_in, from_left, from_right, gather, remote, inverse, inside, out):
    out[...] = joined(q_in, from_left, from_right, gather, remote, inverse, inside)


def call(kernel, shapes, args, name):
    return pl.pallas_call(
        kernel,
        out_shape=tuple(jax.ShapeDtypeStruct(s, t) for s, t in shapes),
        in_specs=[vmem] * len(args),
        out_specs=tuple(vmem for _ in shapes),
        compiler_params=params,
        name=name,
    )(*args)


def shards(
    cloud_state,
    substeps,
    element_links,
    host_state,
    wind_field,
    node_mass,
    field_coupling,
    force_map,
    feedback_map,
):
    own_rows, n_fields, n_cells = cloud_state.shape
    n_vars, lev_dev, n_nodes = host_state.shape
    n_cols = substeps.shape[0]
    elem_dev = n_nodes // 16
    edge = n_nodes // 4
    lev_count = lax.axis_size("lev")
    elem_count = lax.axis_size("elem")
    lev_at = lax.axis_index("lev")
    elem_at = lax.axis_index("elem")
    n_levels = lev_dev * lev_count

    node_ids = jnp.arange(n_nodes)
    column_of_node = node_ids // 16 * 4 + node_ids // 4 % 4 // 2 * 2 + node_ids % 4 // 2
    member = (column_of_node[:, None] == jnp.arange(n_cols)[None, :]).astype(f32)
    host_columns = (
        jnp.dot(host_state.reshape(n_vars * lev_dev, n_nodes), 0.25 * member, precision=highest)
        .reshape(n_vars, lev_dev, n_cols)
        .transpose(2, 0, 1)
    )
    columns = lax.all_to_all(
        host_columns.reshape(lev_count, own_rows, n_vars, lev_dev),
        "lev",
        split_axis=0,
        concat_axis=3,
        tiled=True,
    ).reshape(own_rows, n_vars, n_levels)
    counts = lax.dynamic_slice_in_dim(substeps, lev_at * own_rows, own_rows, 0)

    fields = jnp.concatenate([host_state, wind_field], axis=0)
    up = [(i, i + 1) for i in range(lev_count - 1)]
    down = [(i + 1, i) for i in range(lev_count - 1)]
    fields = jnp.concatenate(
        [
            lax.ppermute(fields[:, lev_dev - HALO :], "lev", up),
            fields,
            lax.ppermute(fields[:, :HALO], "lev", down),
        ],
        axis=1,
    )
    deep = lev_dev + 2 * HALO
    rows = n_vars * deep
    h0 = fields[:n_vars].reshape(rows, n_nodes)
    wind = jnp.tile(fields[n_vars:], (1, n_vars, 1))
    level = lev_at * lev_dev - HALO + jnp.arange(rows) % deep
    inside = jnp.broadcast_to(
        ((level >= 0) & (level < n_levels)).astype(f32)[:, None], (rows, LANES)
    )
    rightward = [(i, (i + 1) % elem_count) for i in range(elem_count)]
    leftward = [((i + 1) % elem_count, i) for i in range(elem_count)]
    masses = jnp.concatenate(
        [
            node_mass[None],
            lax.ppermute(node_mass[None], "elem", rightward),
            lax.ppermute(node_mass[None], "elem", leftward),
            jnp.zeros((5, n_nodes), f32),
        ],
        axis=0,
    )

    ids = jnp.arange(n_nodes, dtype=jnp.int32)
    row_of, col_of = ids // 4 % 4, ids % 4
    links = jnp.repeat(element_links.T, 16, axis=1)
    here = links // elem_dev == elem_at
    place = links % elem_dev
    side_own = jnp.where(
        (col_of == 0) & here[0],
        place[0] * 16 + row_of * 4 + 3,
        jnp.where((col_of == 3) & here[1], place[1] * 16 + row_of * 4, -1),
    )
    side_left = jnp.where((col_of == 0) & ~here[0], place[0] * 4 + row_of, -1)
    side_right = jnp.where((col_of == 3) & ~here[1], place[1] * 4 + row_of, -1)
    vert = jnp.where(
        row_of == 0,
        place[2] * 16 + 12 + col_of,
        jnp.where(row_of == 3, place[3] * 16 + col_of, -1),
    )
    none = jnp.full_like(vert, -1)
    sources = jnp.stack([side_own, side_left, side_right, vert, none, none, none, none])
    gather, remote, inverse = call(
        functools.partial(tables_kernel, elem_dev=elem_dev),
        [((n_nodes, n_nodes), bf16), ((2 * edge, n_nodes), bf16), ((8, n_nodes), f32)],
        (sources, masses),
        "tables",
    )

    cloud_new, tend = run_clouds(
        cloud_state, columns, counts, field_coupling, force_map, feedback_map
    )

    padded = jnp.pad(tend, ((0, 0), (0, 0), (HALO, HALO)))
    blocks = jnp.stack(
        [padded[:, :, k * lev_dev : k * lev_dev + deep] for k in range(lev_count)]
    )
    column = (
        lax.all_to_all(blocks, "lev", split_axis=0, concat_axis=0, tiled=True)
        .reshape(n_cols, rows)
        .T
    )

    derivative = gll_derivative()
    elems = LANES // 16
    derive = np.concatenate(
        [
            np.kron(np.eye(elems * 4), derivative).T,
            np.kron(np.eye(elems), np.kron(derivative, np.eye(4))).T,
        ],
        axis=1,
    ).astype(np.float32)
    d_hi = derive.astype(ml_dtypes.bfloat16)
    d_lo = (derive - d_hi.astype(np.float32)).astype(ml_dtypes.bfloat16)
    derive = jnp.asarray(np.concatenate([d_hi, d_lo], axis=0))

    q_shapes = [((rows, n_nodes), f32), ((rows, edge), f32), ((rows, edge), f32)]
    q, to_right, to_left, physics = call(
        first_kernel,
        q_shapes + [((rows, n_nodes), f32)],
        (h0, wind, column, masses, derive),
        "first",
    )
    for keep, take in ((0.75, 0.25), (1.0 / 3.0, 2.0 / 3.0)):
        from_left = lax.ppermute(to_right, "elem", rightward)
        from_right = lax.ppermute(to_left, "elem", leftward)
        q, to_right, to_left = call(
            functools.partial(middle_kernel, keep=keep, take=take),
            q_shapes,
            (q, from_left, from_right, gather, remote, inverse, inside, h0, wind, physics, masses,
             derive),
            "middle",
        )
    from_left = lax.ppermute(to_right, "elem", rightward)
    from_right = lax.ppermute(to_left, "elem", leftward)
    (last,) = call(
        last_kernel,
        [((rows, n_nodes), f32)],
        (q, from_left, from_right, gather, remote, inverse, inside),
        "last",
    )
    host_new = last.reshape(n_vars, deep, n_nodes)[:, HALO : HALO + lev_dev]
    return (cloud_new, host_new)


def solution(mesh):
    placed = (
        P(("elem", "lev"), None, None),
        P("elem"),
        P("elem", None),
        P(None, "lev", "elem"),
        P(None, "lev", "elem"),
        P("elem"),
        P(),
        P(),
        P(),
    )
    return jax.shard_map(
        shards,
        mesh=mesh,
        in_specs=placed,
        out_specs=(P(("elem", "lev"), None, None), P(None, "lev", "elem")),
        check_vma=False,
    )
```

time: 1460 us -> 450 us (0.31)
  starting transfers between devices: 818 us -> 255 us
  local copies, waits for them, and re-layouts: 340 us -> 18.7 us
  other arithmetic: 177 us -> 4.04 us
  Pallas kernels: 0 us -> 159 us
  matrix products: 97.9 us -> 1.28 us
    ppermute x14 -> x10, starting transfers between devices: 811 us -> 249 us  [the longest x3 232 us: shards(): from_left = lax.ppermute(to_right, 'elem', rightward)]
    pallas_call x0 -> x6, Pallas kernels: none -> 159 us  [the longest x1 154 us: run_clouds(): pl.pallas_call(cloud_kernel, out_shape=(jax.ShapeDtypeStruct((rows, n_cel...]
    slice x15 -> x3, local copies, waits for them, and re-layouts: 111 us -> 0.71 us  [the longest x1 0.67 us: shards(): host_new = last.reshape(n_vars, deep, n_nodes)[:, HALO:HALO + lev_dev]]
    reshape x16 -> x3, local copies, waits for them, and re-layouts: 103 us -> 0.33 us  [the longest x1 0.14 us: shards(): column = lax.all_to_all(blocks, 'lev', split_axis=0, concat_axis=0, tiled...]
    dot_general x28 -> x1, matrix products: 97.9 us -> 1.28 us  [shards(): jnp.dot(host_state.reshape(n_vars * lev_dev, n_nodes), 0.25 * member, pre...]
    add x9 -> x0, other arithmetic: 79.4 us -> none  [the longest x6 79.4 us: one_step(): eastward + westward - 2.0 * current]
    select_n x2 -> x5, other arithmetic: 63.8 us -> 0.5 us  [the longest x3 0.46 us: spread_diagonal(): return jnp.where(row == col, tiled, 0.0)]
    add x6 -> x0, local copies, waits for them, and re-layouts: 47.4 us -> none  [one_step(): eastward + westward - 2.0 * current]
  transfers between devices with their start and end apart: 16 -> 12, of which waited for: 6 -> 6; matrix products, arithmetic and copies ran while one was open for 42% -> 4% of each run, Pallas kernels for 0% -> 35%
where the time goes in v1:
time: 450 us
  starting transfers between devices  255 us (57%)
  Pallas kernels  159 us (35%)
  local copies, waits for them, and re-layouts  18.7 us (4%)
  waiting for transfers between devices  11.2 us (2%)
    ppermute x3, starting transfers between devices, shards(): from_left = lax.ppermute(to_right, 'elem', rightward)  232 us
    pallas_call x1, Pallas kernels, run_clouds(): pl.pallas_call(cloud_kernel, out_shape=(jax.ShapeDtypeStruct((rows, n_cel...  154 us
    another operation x7, local copies, waits for them, and re-layouts, spread_diagonal(): tiled = jnp.tile(matrix, (count, count))  10.3 us
  transfers between devices with their start and end apart: 12, of which 6 were waited for; matrix products, arithmetic and copies ran while one was open for 4% of the time, Pallas kernels for 35%

profile of v1, /device:TPU:0, one launch (start us, length us, event | category | flops | bytes accessed | tf_op | source)
XLA Modules:
  0.0 450.1 jit_solution(4041589509505430462)
XLA Ops:
  0.6 6.0 %collective-permute-start.3 = (f32[1,512]{1,0:T(1,128)}, f32[1,512]{1,0:T(1,128)S(1)}, u32[]{:S(2)}, u32[]{:S(2)}) collective-permute-start(f32[1,512]{1,0:T(1,128)} %bitcast.65), channel_id=1, source_target_pairs={{4,0},{8,4},{12,8},{16,12},{20,16},{24,20},{28,24},{0,28},{5,1},{9... | collective-permute-start | bytes 6152 | tf_op jit(solution)/shard_map/ppermute | solution.py:407
  6.7 1.3 fusion
  8.0 0.1 reshape.235
  8.1 0.7 reshape.242
  8.8 3.3 all-to-all-start
  12.1 0.9 constant_dynamic-update-slice_fusion.1
  13.0 0.8 constant_dynamic-update-slice_fusion
  13.9 1.3 collective-permute-start.1
  15.2 3.0 collective-permute-start
  18.3 0.0 copy-start.2
  18.3 3.2 tile.16
  21.5 4.0 tile.17
  25.6 0.2 tile.18
  25.8 0.0 copy-start.4
  25.9 0.0 copy-start.5
  25.9 1.2 tile.19
  27.1 0.1 copy.23
  27.2 0.2 tile.40
  27.4 1.2 tile.41
  28.7 0.2 fusion.2.kron
  28.8 0.2 fusion.6.force
  29.0 0.1 fusion.7.feed
  29.1 0.1 broadcast_in_dim.54
  29.2 0.1 reshape.240
  29.4 0.7 fusion.36
  30.1 1.3 pad_add_fusion.ends
  31.4 0.1 broadcast_in_dim.46
  31.5 0.1 broadcast_in_dim.47
  31.6 0.1 pad.8.clone
  31.7 0.1 maximum_maximum_fusion.mass.masses
  31.8 0.5 broadcast.695
  32.3 0.6 reduce
  32.9 0.1 reshape.243
  33.0 0.2 copy.25
  33.2 0.2 reshape_reshape.3.columns
  33.4 0.1 broadcast_in_dim.48.row_counts
  33.5 0.0 copy-start.1
  33.5 2.2 copy-done.1
  35.7 154.4 %clouds.1 = (f32[256,4096]{1,0:T(8,128)}, f32[128,64]{1,0:T(8,128)S(1)}) custom-call(s32[2]{0:T(128)S(1)} %pad_add_fusion.ends, s32[256,128]{1,0:T(8,128)S(1)} %broadcast_in_dim.48.row_counts, f32[256,4096]{1,0:T(8,128)S(1)} %bitcast.59, f32[256,256]{1,0:T(8,128)S(1)} %fusion.2.kron, f32[256,128]{1,0:T(8,128)S(1)} %fusion.6.force, ...), custom_call_target="tpu_custom_call" | custom-call | flops 25769803776 | bytes 8388608 | tf_op jit(solution)/shard_map/clouds/pallas_call | solution.py:199
  190.1 0.1 copy.26
  190.2 0.8 reshape.244
  191.0 3.3 all-to-all-start.1
  194.4 3.9 all-to-all-done.1
  198.3 0.7 reduce.1
  198.9 0.1 reshape.245
  199.1 0.1 copy.29
  199.2 0.1 reshape.239
  199.4 0.6 first.1
  200.0 0.1 collective-permute-start.4
  200.1 4.9 %collective-permute-start.5 = (f32[96,128]{1,0:T(8,128)S(1)}, f32[96,128]{1,0:T(8,128)S(1)}, u32[]{:S(2)}, u32[]{:S(2)}) collective-permute-start(f32[96,128]{1,0:T(8,128)S(1)} %get-tuple-element.21), channel_id=1, source_target_pairs={{4,0},{8,4},{12,8},{16,12},{20,16},{24,20},{28,24},{0,28},{5,1},{9... | collective-permute-start | bytes 147464 | tf_op jit(solution)/shard_map/ppermute | solution.py:475
  205.1 1.1 tables.1
  206.2 0.7 collective-permute-done.4.from_left
  206.9 0.1 broadcast_in_dim.55.inside
  207.0 1.0 middle.2
  208.0 228.6 %collective-permute-start.6 = (f32[96,128]{1,0:T(8,128)S(1)}, f32[96,128]{1,0:T(8,128)S(1)}, u32[]{:S(2)}, u32[]{:S(2)}) collective-permute-start(f32[96,128]{1,0:T(8,128)S(1)} %get-tuple-element.27), channel_id=1, source_target_pairs={{0,4},{4,8},{8,12},{12,16},{16,20},{20,24},{24,28},{28,0},{1,5},{5... | collective-permute-start | bytes 147464 | tf_op jit(solution)/shard_map/ppermute | solution.py:474
  436.6 2.1 collective-permute-done.6.from_left
  438.6 2.0 collective-permute-done.7.from_right
  440.6 1.0 middle.3
  441.6 3.0 collective-permute-start.8
  444.6 1.8 collective-permute-start.9
  446.4 2.1 collective-permute-done.8.from_left
  448.5 0.5 collective-permute-done.9.from_right
  449.0 0.4 last.1
  449.4 0.7 slice.77
  (38 shorter events, 0.4 us)
Async XLA Ops:
  0.6 31.0 %collective-permute-start.3 = (f32[1,512]{1,0:T(1,128)}, f32[1,512]{1,0:T(1,128)S(1)}, u32[]{:S(2)}, u32[]{:S(2)}) collective-permute-start(f32[1,512]{1,0:T(1,128)} %bitcast.65), channel_id=1, source_target_pairs={{4,0},{8,4},{12,8},{16,12},{20,16},{24,20},{28,24},{0,28},{5,1},{9... | collective-permute-start | bytes 6152 | tf_op jit(solution)/shard_map/ppermute | solution.py:407
  6.7 25.0 %collective-permute-start.2 = (f32[1,512]{1,0:T(1,128)}, f32[1,512]{1,0:T(1,128)S(1)}, u32[]{:S(2)}, u32[]{:S(2)}) collective-permute-start(f32[1,512]{1,0:T(1,128)} %bitcast.66), channel_id=1, source_target_pairs={{0,4},{4,8},{8,12},{12,16},{16,20},{20,24},{24,28},{28,0},{1,5},{5... | collective-permute-start | bytes 6152 | tf_op jit(solution)/shard_map/ppermute | solution.py:406
  8.8 22.9 %all-to-all-start = ((f32[4,1,2048]{2,1,0:T(1,128)}), f32[4,1,2048]{2,1,0:T(1,128)S(1)}, u32[]{:S(2)}, u32[]{:S(2)}) async-start(f32[4,1,2048]{2,1,0:T(1,128)} %reshape.242), calls=%async_computation | async-start | bytes 65536 | tf_op jit(solution)/shard_map/all_to_all | solution.py:373
  13.9 180.4 %collective-permute-start.1 = (f32[6,4,512]{2,1,0:T(4,128)S(1)}, f32[6,4,512]{2,1,0:T(4,128)S(1)}, u32[]{:S(2)}, u32[]{:S(2)}) collective-permute-start(f32[6,4,512]{2,1,0:T(4,128)S(1)} %get-tuple-element.36), channel_id=1, source_target_pairs={{1,0},{2,1},{3,2},{5,4},{6,5},{7,6},{9,8},{10,9},{11,10},{13,12},{... | collective-permute-start | bytes 147464 | tf_op jit(solution)/shard_map/ppermute | solution.py:389
  15.2 179.1 %collective-permute-start = (f32[6,4,512]{2,1,0:T(4,128)S(1)}, f32[6,4,512]{2,1,0:T(4,128)S(1)}, u32[]{:S(2)}, u32[]{:S(2)}) collective-permute-start(f32[6,4,512]{2,1,0:T(4,128)S(1)} %get-tuple-element.35), channel_id=1, source_target_pairs={{0,1},{1,2},{2,3},{4,5},{5,6},{6,7},{8,9},{9,10},{10,11},{12,13},{... | collective-permute-start | bytes 147464 | tf_op jit(solution)/shard_map/ppermute | solution.py:387
  18.3 7.3 %copy-start.2 = (f32[8,4]{0,1:T(4,128)S(1)}, f32[8,4]{0,1:T(4,128)}, u32[]{:S(2)}) copy-start(f32[8,4]{0,1:T(4,128)} %param.17) | copy-start | bytes 388
  21.5 5.6 %copy-start.3 = (f32[4,8]{1,0:T(4,128)S(1)}, f32[4,8]{1,0:T(4,128)}, u32[]{:S(2)}) copy-start(f32[4,8]{1,0:T(4,128)} %param.18) | copy-start | bytes 388
  25.8 3.3 copy-start.4
  25.8 3.5 copy-start.6
  25.9 5.8 %copy-start.5 = (f32[512]{0:T(512)S(1)}, f32[512]{0:T(512)}, u32[]{:S(2)}) copy-start(f32[512]{0:T(512)} %param.15) | copy-start | bytes 6148
  33.5 2.2 copy-start.1
  190.0 9.3 %copy-start = (bf16[256,256]{1,0:T(8,128)(2,1)S(1)}, bf16[256,256]{1,0:T(8,128)(2,1)}, u32[]{:S(2)}) copy-start(bf16[256,256]{1,0:T(8,128)(2,1)} %constant.236.clone.derive) | copy-start | bytes 393220
  191.0 7.3 %all-to-all-start.1 = ((f32[4,1,3072]{2,1,0:T(1,128)}), f32[4,1,3072]{2,1,0:T(1,128)S(1)}, u32[]{:S(2)}, u32[]{:S(2)}) async-start(f32[4,1,3072]{2,1,0:T(1,128)} %reshape.244), calls=%async_computation.1 | async-start | bytes 98304 | tf_op jit(solution)/shard_map/all_to_all | solution.py:448
  200.0 6.8 %collective-permute-start.4 = (f32[96,128]{1,0:T(8,128)S(1)}, f32[96,128]{1,0:T(8,128)S(1)}, u32[]{:S(2)}, u32[]{:S(2)}) collective-permute-start(f32[96,128]{1,0:T(8,128)S(1)} %get-tuple-element.20), channel_id=1, source_target_pairs={{0,4},{4,8},{8,12},{12,16},{16,20},{20,24},{24,28},{28,0},{1,5},{5... | collective-permute-start | bytes 147464 | tf_op jit(solution)/shard_map/ppermute | solution.py:474
  200.1 6.8 %collective-permute-start.5 = (f32[96,128]{1,0:T(8,128)S(1)}, f32[96,128]{1,0:T(8,128)S(1)}, u32[]{:S(2)}, u32[]{:S(2)}) collective-permute-start(f32[96,128]{1,0:T(8,128)S(1)} %get-tuple-element.21), channel_id=1, source_target_pairs={{4,0},{8,4},{12,8},{16,12},{20,16},{24,20},{28,24},{0,28},{5,1},{9... | collective-permute-start | bytes 147464 | tf_op jit(solution)/shard_map/ppermute | solution.py:475
  208.0 230.7 %collective-permute-start.6 = (f32[96,128]{1,0:T(8,128)S(1)}, f32[96,128]{1,0:T(8,128)S(1)}, u32[]{:S(2)}, u32[]{:S(2)}) collective-permute-start(f32[96,128]{1,0:T(8,128)S(1)} %get-tuple-element.27), channel_id=1, source_target_pairs={{0,4},{4,8},{8,12},{12,16},{16,20},{20,24},{24,28},{28,0},{1,5},{5... | collective-permute-start | bytes 147464 | tf_op jit(solution)/shard_map/ppermute | solution.py:474
  436.5 4.1 collective-permute-start.7
  441.6 6.9 %collective-permute-start.8 = (f32[96,128]{1,0:T(8,128)S(1)}, f32[96,128]{1,0:T(8,128)S(1)}, u32[]{:S(2)}, u32[]{:S(2)}) collective-permute-start(f32[96,128]{1,0:T(8,128)S(1)} %get-tuple-element.30), channel_id=1, source_target_pairs={{0,4},{4,8},{8,12},{12,16},{16,20},{20,24},{24,28},{28,0},{1,5},{5... | collective-permute-start | bytes 147464 | tf_op jit(solution)/shard_map/ppermute | solution.py:483
  444.6 4.4 collective-permute-start.9

commit v2 on v1

--- a/solution.py
+++ b/solution.py
@@ -13,6 +13,8 @@
 HALO = 4
 LANES = 128
 PAIR = 256
+GROUP = 32
+UNROLL = 2
 
 mix = 0.2
 cloud_step = 0.1
@@ -59,12 +61,6 @@
     return mm(hi, b) + mm(lo, b)
 
 
-def dot3(a, b):
-    a_hi, a_lo = split(a)
-    b_hi, b_lo = split(b)
-    return mm(a_hi, b_hi) + mm(a_hi, b_lo) + mm(a_lo, b_hi)
-
-
 def iota(shape, dim):
     return lax.broadcasted_iota(jnp.int32, shape, dim)
 
@@ -73,31 +69,41 @@
     return jnp.where(cond, 1.0, 0.0).astype(bf16)
 
 
+def diagonal(matrix, height, width, part, rows, cols):
+    piece = split(matrix[...])[part]
+    down = one_hot(iota((rows, LANES), 1) == iota((rows, LANES), 0) % height)
+    along = one_hot(iota((LANES, cols), 0) == iota((LANES, cols), 1) % width)
+    tiled = mm(mm(down, piece).astype(bf16), along)
+    same = iota((rows, cols), 0) // height == iota((rows, cols), 1) // width
+    return jnp.where(same, tiled, 0.0).astype(bf16)
+
+
 def cloud_kernel(
-    ends, row_counts, cells, kron, force, feed, columns, out, tend,
-    state, spread, k_wide, k_low, parts, change,
+    fields, n_vars, ends, row_counts, cells, kron, force, feed, columns, out, tend,
+    state, other, spread, k_wide, k_low, change,
 ):
     rows, n_cells = cells.shape
     half = n_cells // 2
     levels = n_cells // CRM_X
     blocks = half // LANES
-    group = 32
-
-    k_hi, k_lo = split(kron[...])
+    k_hi, k_lo = (diagonal(kron, fields, fields, part, rows, rows) for part in (0, 1))
     k_wide[:, :rows] = k_hi
     k_wide[:, rows:] = k_hi
     k_low[...] = k_lo
-    driving = cloud_step * dot3(force[...], columns[...])
+    wide = columns.shape[0]
+    f_hi, f_lo = (diagonal(force, fields, n_vars, part, rows, wide) for part in (0, 1))
+    c_hi, c_lo = split(columns[...])
+    driving = cloud_step * (mm(f_hi, c_hi) + mm(f_hi, c_lo) + mm(f_lo, c_hi))
     src, dst = iota((PAIR, PAIR), 0), iota((PAIR, PAIR), 1)
     weave = one_hot(src == dst % 2 * LANES + dst // LANES * CRM_X + dst % LANES // 2)
     unweave = one_hot(dst == src % 2 * LANES + src // LANES * CRM_X + src % LANES // 2)
     odd = iota((rows, LANES), 1) % 2 == 1
 
-    def ends_of(slot):
-        last = state[slot, :, pl.ds(half * 2, LANES)]
-        first = state[slot, :, pl.ds(LANES, LANES)]
-        state[slot, :, pl.ds(0, LANES)] = jnp.where(odd, pltpu.roll(last, 1, 1), 0.0)
-        state[slot, :, pl.ds(half * 2 + LANES, LANES)] = jnp.where(
+    def ends_of(ref):
+        last = ref[:, pl.ds(half * 2, LANES)]
+        first = ref[:, pl.ds(LANES, LANES)]
+        ref[:, pl.ds(0, LANES)] = jnp.where(odd, pltpu.roll(last, 1, 1), 0.0)
+        ref[:, pl.ds(half * 2 + LANES, LANES)] = jnp.where(
             odd, 0.0, pltpu.roll(first, LANES - 1, 1)
         )
 
@@ -108,7 +114,7 @@
 
     def enter(k, carry):
         at = pl.multiple_of(k * PAIR, LANES)
-        state[0, :, pl.ds(pl.multiple_of(at + LANES, LANES), PAIR)] = dot_exact_right(
+        state[:, pl.ds(pl.multiple_of(at + LANES, LANES), PAIR)] = dot_exact_right(
             pair_of(cells, k), weave
         )
         lane = iota((levels, PAIR), 1)
@@ -118,56 +124,57 @@
         )
         return carry
 
-    lax.fori_loop(0, blocks, enter, 0)
-    ends_of(0)
-
-    def step_of(masked):
-        def step(s, carry):
-            now = s % 2
-            later = 1 - now
-
-            def block(k, inner):
-                at = pl.multiple_of(k * PAIR, LANES)
-                mid = pl.multiple_of(at + LANES, LANES)
-                for g in range(0, rows, group):
-                    hi, lo = split(state[now, pl.ds(g, group), pl.ds(mid, PAIR)])
-                    parts[pl.ds(g, group), :] = hi
-                    parts[pl.ds(rows + g, group), :] = lo
-                react = mm(k_wide[...], parts[...]) + mm(k_low[...], parts[pl.ds(0, rows), :])
-                for g in range(0, rows, group):
-                    for c in range(0, PAIR, LANES):
-                        take = lambda start: state[
-                            now, pl.ds(g, group), pl.ds(pl.multiple_of(start, LANES), LANES)
-                        ]
-                        x = take(mid + c)
-                        total = (x + (take(at + c) + take(mid + c + LANES))) + (
-                            pltpu.roll(x, 2, 1) + pltpu.roll(x, LANES - 2, 1)
-                        )
-                        drive = spread[pl.ds(g, group), pl.ds(pl.multiple_of(at + c, LANES), LANES)]
-                        new = mix * total + (
-                            cloud_step * jnp.tanh(react[g : g + group, c : c + LANES]) + drive
-                        )
-                        if masked:
-                            new = jnp.where(s < row_counts[pl.ds(g, group), :], new, x)
-                        state[
-                            later, pl.ds(g, group), pl.ds(pl.multiple_of(mid + c, LANES), LANES)
-                        ] = new
-                return inner
-
-            lax.fori_loop(0, blocks, block, 0)
-            ends_of(later)
+    lax.fori_loop(0, blocks, enter, 0, unroll=UNROLL)
+    ends_of(state)
+
+    def step(now, later, s, masked):
+        def block(k, inner):
+            at = pl.multiple_of(k * PAIR, LANES)
+            mid = pl.multiple_of(at + LANES, LANES)
+            hi, lo = split(now[:, pl.ds(mid, PAIR)])
+            react = mm(k_wide[...], jnp.concatenate([hi, lo], axis=0)) + mm(k_low[...], hi)
+            for g in range(0, rows, GROUP):
+                own = pl.ds(g, min(GROUP, rows))
+                x = now[own, pl.ds(mid, PAIR)]
+                beside = jnp.concatenate(
+                    [
+                        pltpu.roll(x[:, c : c + LANES], 2, 1)
+                        + pltpu.roll(x[:, c : c + LANES], LANES - 2, 1)
+                        for c in range(0, PAIR, LANES)
+                    ],
+                    axis=1,
+                )
+                below = now[own, pl.ds(at, PAIR)]
+                above = now[own, pl.ds(pl.multiple_of(mid + LANES, LANES), PAIR)]
+                total = (x + (below + above)) + beside
+                new = mix * total + (
+                    cloud_step * jnp.tanh(react[g : g + GROUP]) + spread[own, pl.ds(at, PAIR)]
+                )
+                if masked:
+                    alive = s < row_counts[own, :]
+                    new = jnp.where(jnp.concatenate([alive] * (PAIR // LANES), axis=1), new, x)
+                later[own, pl.ds(mid, PAIR)] = new
+            return inner
+
+        lax.fori_loop(0, blocks, block, 0, unroll=UNROLL)
+        ends_of(later)
+
+    def steps_of(masked):
+        def two(pair, carry):
+            step(state, other, 2 * pair, masked)
+            step(other, state, 2 * pair + 1, masked)
             return carry
 
-        return step
-
-    lax.fori_loop(0, ends[0], step_of(False), 0)
-    lax.fori_loop(ends[0], ends[1], step_of(True), 0)
-    final = ends[1] % 2
+        return two
+
+    full = ends[0] // 2
+    lax.fori_loop(0, full, steps_of(False), 0)
+    lax.fori_loop(full, (ends[1] + 1) // 2, steps_of(True), 0)
     change[...] = jnp.zeros_like(change)
 
     def leave(k, carry):
         at = pl.multiple_of(k * PAIR + LANES, LANES)
-        new = dot_exact_right(state[final, :, pl.ds(at, PAIR)], unweave)
+        new = dot_exact_right(state[:, pl.ds(at, PAIR)], unweave)
         delta = new - pair_of(cells, k)
         out[:, pl.ds(pl.multiple_of(k * LANES, LANES), LANES)] = new[:, :LANES]
         out[:, pl.ds(pl.multiple_of(half + k * LANES, LANES), LANES)] = new[:, LANES:]
@@ -177,16 +184,15 @@
         change[...] += dot_exact_right(delta, mean)
         return carry
 
-    lax.fori_loop(0, blocks, leave, 0)
-    tend[...] = dot3(feed[...], change[...])
-
-
-def spread_diagonal(matrix, count):
+    lax.fori_loop(0, blocks, leave, 0, unroll=UNROLL)
+    b_hi, b_lo = (diagonal(feed, n_vars, fields, part, wide, rows) for part in (0, 1))
+    d_hi, d_lo = split(change[...])
+    tend[...] = mm(b_hi, d_hi) + mm(b_hi, d_lo) + mm(b_lo, d_hi)
+
+
+def square(matrix):
     height, width = matrix.shape
-    tiled = jnp.tile(matrix, (count, count))
-    row = iota(tiled.shape, 0) // height
-    col = iota(tiled.shape, 1) // width
-    return jnp.where(row == col, tiled, 0.0)
+    return jnp.pad(matrix, ((0, LANES - height), (0, LANES - width)))
 
 
 def run_clouds(cloud_state, columns, counts, coupling, force_map, feedback_map):
@@ -197,7 +203,7 @@
     ends = jnp.stack([jnp.min(counts), jnp.max(counts)])
     row_counts = jnp.broadcast_to(counts[:, None, None], (own, n_fields, LANES))
     out, tend = pl.pallas_call(
-        cloud_kernel,
+        functools.partial(cloud_kernel, n_fields, n_vars),
         out_shape=(
             jax.ShapeDtypeStruct((rows, n_cells), f32),
             jax.ShapeDtypeStruct((own * n_vars, levels), f32),
@@ -205,11 +211,11 @@
         in_specs=[smem] + [vmem] * 6,
         out_specs=(vmem, vmem),
         scratch_shapes=[
-            pltpu.VMEM((2, rows, n_cells + 2 * LANES), f32),
+            pltpu.VMEM((rows, n_cells + 2 * LANES), f32),
+            pltpu.VMEM((rows, n_cells + 2 * LANES), f32),
             pltpu.VMEM((rows, n_cells), f32),
             pltpu.VMEM((rows, 2 * rows), bf16),
             pltpu.VMEM((rows, rows), bf16),
-            pltpu.VMEM((2 * rows, PAIR), bf16),
             pltpu.VMEM((rows, levels), f32),
         ],
         compiler_params=params,
@@ -223,9 +229,9 @@
         ends,
         row_counts.reshape(rows, LANES),
         cloud_state.reshape(rows, n_cells),
-        spread_diagonal(coupling, own),
-        spread_diagonal(force_map, own),
-        spread_diagonal(feedback_map, own),
+        square(coupling),
+        square(force_map),
+        square(feedback_map),
         columns.reshape(own * n_vars, levels),
     )
     return out.reshape(cloud_state.shape), tend.reshape(own, n_vars, levels)

time: 450 us -> 150 us (0.33)
  starting transfers between devices: 255 us -> 73.2 us
  Pallas kernels: 159 us -> 46.4 us
  local copies, waits for them, and re-layouts: 18.7 us -> 11.2 us
    ppermute x3, starting transfers between devices: 232 us -> 48.5 us  [shards(): from_left = lax.ppermute(to_right, 'elem', rightward)]
    pallas_call x1, Pallas kernels: 154 us -> 42.2 us  [run_clouds(): pl.pallas_call(functools.partial(cloud_kernel, n_fields, n_vars), out_sha...]
    another operation x8 -> x1, local copies, waits for them, and re-layouts: 10.3 us -> 0.01 us  [shards(): node_ids // 16 * 4 + node_ids // 4 % 4 // 2 * 2 + node_ids % 4 // 2]
  transfers between devices with their start and end apart: 12 -> 12, of which waited for: 6 -> 6; matrix products, arithmetic and copies ran while one was open for 4% -> 9% of each run, Pallas kernels for 35% -> 29%
where the time goes in v2:
time: 150 us; the launch traced here: 149 us
  starting transfers between devices  73.2 us (49%)
  Pallas kernels  46.4 us (31%)
  waiting for transfers between devices  11.4 us (8%)
  local copies, waits for them, and re-layouts  11.2 us (7%)
  other arithmetic  4.92 us (3%)
    ppermute x3, starting transfers between devices, shards(): from_left = lax.ppermute(to_right, 'elem', rightward)  48.5 us
    pallas_call x1, Pallas kernels, run_clouds(): pl.pallas_call(functools.partial(cloud_kernel, n_fields, n_vars), out_sha...  42.2 us
    ppermute x3, starting transfers between devices, shards(): from_right = lax.ppermute(to_left, 'elem', leftward)  6.57 us
    ppermute x1, starting transfers between devices, shards(): lax.ppermute(node_mass[None], 'elem', leftward)  6.03 us
    unnamed x10, local copies, waits for them, and re-layouts  5.57 us
    all_to_all x1, starting transfers between devices, shards(): lax.all_to_all(blocks, 'lev', split_axis=0, concat_axis=0, tiled=True)  5.17 us
    ppermute x3, waiting for transfers between devices, shards(): from_left = lax.ppermute(to_right, 'elem', rightward)  5.02 us
    pallas_call x5, Pallas kernels, call(): pl.pallas_call(kernel, out_shape=tuple((jax.ShapeDtypeStruct(s, t) for s,...  4.14 us
  transfers between devices with their start and end apart: 12, of which 6 were waited for; matrix products, arithmetic and copies ran while one was open for 9% of the time, Pallas kernels for 29%

profile of v2, /device:TPU:0, one launch (start us, length us, event | category | flops | bytes accessed | tf_op | source)
XLA Modules:
  0.0 149.4 jit_solution(17454803182698358984)
XLA Ops:
  0.6 6.0 %collective-permute-start.3 = (f32[1,512]{1,0:T(1,128)}, f32[1,512]{1,0:T(1,128)S(1)}, u32[]{:S(2)}, u32[]{:S(2)}) collective-permute-start(f32[1,512]{1,0:T(1,128)} %bitcast.57), channel_id=1, source_target_pairs={{4,0},{8,4},{12,8},{16,12},{20,16},{24,20},{28,24},{0,28},{5,1},{9... | collective-permute-start | bytes 6152 | tf_op jit(solution)/shard_map/ppermute | solution.py:413
  6.7 0.0 collective-permute-start.2
  6.7 1.3 fusion
  8.0 0.1 reshape.232
  8.1 0.7 reshape.239
  8.8 3.3 %all-to-all-start = ((f32[4,1,2048]{2,1,0:T(1,128)}), f32[4,1,2048]{2,1,0:T(1,128)S(1)}, u32[]{:S(2)}, u32[]{:S(2)}) async-start(f32[4,1,2048]{2,1,0:T(1,128)} %reshape.239), calls=%async_computation | async-start | bytes 65536 | tf_op jit(solution)/shard_map/all_to_all | solution.py:379
  12.1 0.9 constant_dynamic-update-slice_fusion.1
  13.0 0.8 constant_dynamic-update-slice_fusion
  13.9 2.4 %collective-permute-start = (f32[6,4,512]{2,1,0:T(4,128)S(1)}, f32[6,4,512]{2,1,0:T(4,128)S(1)}, u32[]{:S(2)}, u32[]{:S(2)}) collective-permute-start(f32[6,4,512]{2,1,0:T(4,128)S(1)} %get-tuple-element.35), channel_id=1, source_target_pairs={{0,1},{1,2},{2,3},{4,5},{5,6},{6,7},{8,9},{9,10},{10,11},{12,13},{... | collective-permute-start | bytes 147464 | tf_op jit(solution)/shard_map/ppermute | solution.py:393
  16.3 1.3 collective-permute-start.1
  17.6 0.8 broadcast_in_dim.39
  18.3 0.1 reshape.237
  18.5 1.4 fusion.33
  19.9 1.3 pad_add_fusion.ends
  21.2 0.8 copy.23
  21.9 0.1 broadcast_in_dim.34
  22.0 0.1 broadcast_in_dim.35
  22.1 0.7 pad.16.kron
  22.8 0.7 pad.18.feed
  23.5 0.1 pad.23.clone
  23.6 0.0 collective-permute-done.3
  23.6 0.0 collective-permute-done.2
  23.6 0.8 maximum_maximum_fusion.mass.masses
  24.3 0.0 all-to-all-done
  24.3 0.5 broadcast.566
  24.9 0.6 reduce
  25.5 0.1 reshape.240
  25.6 0.2 copy.25
  25.8 0.2 reshape_reshape.3.columns
  26.0 0.1 broadcast_in_dim.36.row_counts
  26.1 0.0 copy-start.1
  26.1 2.2 %copy-done.1 = f32[32,8,4096]{2,1,0:T(8,128)S(1)} copy-done((f32[32,8,4096]{2,1,0:T(8,128)S(1)}, f32[32,8,4096]{2,1,0:T(8,128)}, u32[]{:S(2)}) %copy-start.1) | copy-done | bytes 4194328
  28.3 42.2 %clouds.1 = (f32[256,4096]{1,0:T(8,128)}, f32[128,64]{1,0:T(8,128)S(1)}) custom-call(s32[2]{0:T(128)S(1)} %pad_add_fusion.ends, s32[256,128]{1,0:T(8,128)S(1)} %broadcast_in_dim.36.row_counts, f32[256,4096]{1,0:T(8,128)S(1)} %bitcast.51, f32[128,128]{1,0:T(8,128)S(1)} %pad.16.kron, f32[128,128]{1,0:T(8,128)S(1)} %pad.17.force, f32[128,128]{1,0:T(8,128)S(1)} %pad.18.feed, ...), custom_call_target="tpu_custom_call" | custom-call | flops 25769803776 | bytes 8388608 | tf_op jit(solution)/shard_map/clouds/pallas_call | solution.py:205
  70.5 0.0 copy-start
  70.5 0.1 copy.26
  70.7 0.8 reshape.241
  71.4 5.2 %all-to-all-start.1 = ((f32[4,1,3072]{2,1,0:T(1,128)}), f32[4,1,3072]{2,1,0:T(1,128)S(1)}, u32[]{:S(2)}, u32[]{:S(2)}) async-start(f32[4,1,3072]{2,1,0:T(1,128)} %reshape.241), calls=%async_computation.1 | async-start | bytes 98304 | tf_op jit(solution)/shard_map/all_to_all | solution.py:454
  76.6 0.0 collective-permute-done
  76.6 0.0 collective-permute-done.1
  76.7 3.9 %all-to-all-done.1 = f32[4,1,3072]{2,1,0:T(1,128)S(1)} async-done(((f32[4,1,3072]{2,1,0:T(1,128)}), f32[4,1,3072]{2,1,0:T(1,128)S(1)}, u32[]{:S(2)}, u32[]{:S(2)}) %all-to-all-start.1) | async-done | bytes 49184 | tf_op jit(solution)/shard_map/all_to_all | solution.py:454
  80.6 0.7 reduce.1
  81.3 0.1 reshape.242
  81.4 0.1 copy.29
  81.6 0.1 reshape.236
  81.8 0.0 copy-done
  81.8 0.6 first.1
  82.4 0.1 collective-permute-start.4
  82.5 4.8 %collective-permute-start.5 = (f32[96,128]{1,0:T(8,128)S(1)}, f32[96,128]{1,0:T(8,128)S(1)}, u32[]{:S(2)}, u32[]{:S(2)}) collective-permute-start(f32[96,128]{1,0:T(8,128)S(1)} %get-tuple-element.21), channel_id=1, source_target_pairs={{4,0},{8,4},{12,8},{16,12},{20,16},{24,20},{28,24},{0,28},{5,1},{9... | collective-permute-start | bytes 147464 | tf_op jit(solution)/shard_map/ppermute | solution.py:481
  87.3 1.1 tables.1
  88.4 0.8 collective-permute-done.4.from_left
  89.3 0.0 collective-permute-done.5.from_right
  89.3 0.1 broadcast_in_dim.40.inside
  89.3 1.0 middle.2
  90.3 45.5 %collective-permute-start.6 = (f32[96,128]{1,0:T(8,128)S(1)}, f32[96,128]{1,0:T(8,128)S(1)}, u32[]{:S(2)}, u32[]{:S(2)}) collective-permute-start(f32[96,128]{1,0:T(8,128)S(1)} %get-tuple-element.27), channel_id=1, source_target_pairs={{0,4},{4,8},{8,12},{12,16},{16,20},{20,24},{24,28},{28,0},{1,5},{5... | collective-permute-start | bytes 147464 | tf_op jit(solution)/shard_map/ppermute | solution.py:480
  135.8 0.0 collective-permute-start.7
  135.8 2.1 %collective-permute-done.6.from_left = f32[96,128]{1,0:T(8,128)S(1)} collective-permute-done((f32[96,128]{1,0:T(8,128)S(1)}, f32[96,128]{1,0:T(8,128)S(1)}, u32[]{:S(2)}, u32[]{:S(2)}) %collective-permute-start.6) | collective-permute-done | bytes 49184 | tf_op jit(solution)/shard_map/ppermute | solution.py:480
  137.9 2.0 %collective-permute-done.7.from_right = f32[96,128]{1,0:T(8,128)S(1)} collective-permute-done((f32[96,128]{1,0:T(8,128)S(1)}, f32[96,128]{1,0:T(8,128)S(1)}, u32[]{:S(2)}, u32[]{:S(2)}) %collective-permute-start.7) | collective-permute-done | bytes 49184 | tf_op jit(solution)/shard_map/ppermute | solution.py:481
  139.9 1.0 middle.3
  140.9 3.0 %collective-permute-start.8 = (f32[96,128]{1,0:T(8,128)S(1)}, f32[96,128]{1,0:T(8,128)S(1)}, u32[]{:S(2)}, u32[]{:S(2)}) collective-permute-start(f32[96,128]{1,0:T(8,128)S(1)} %get-tuple-element.30), channel_id=1, source_target_pairs={{0,4},{4,8},{8,12},{12,16},{16,20},{20,24},{24,28},{28,0},{1,5},{5... | collective-permute-start | bytes 147464 | tf_op jit(solution)/shard_map/ppermute | solution.py:489
  143.9 1.8 %collective-permute-start.9 = (f32[96,128]{1,0:T(8,128)S(1)}, f32[96,128]{1,0:T(8,128)S(1)}, u32[]{:S(2)}, u32[]{:S(2)}) collective-permute-start(f32[96,128]{1,0:T(8,128)S(1)} %get-tuple-element.31), channel_id=1, source_target_pairs={{4,0},{8,4},{12,8},{16,12},{20,16},{24,20},{28,24},{0,28},{5,1},{9... | collective-permute-start | bytes 147464 | tf_op jit(solution)/shard_map/ppermute | solution.py:490
  145.7 2.1 %collective-permute-done.8.from_left = f32[96,128]{1,0:T(8,128)S(1)} collective-permute-done((f32[96,128]{1,0:T(8,128)S(1)}, f32[96,128]{1,0:T(8,128)S(1)}, u32[]{:S(2)}, u32[]{:S(2)}) %collective-permute-start.8) | collective-permute-done | bytes 49184 | tf_op jit(solution)/shard_map/ppermute | solution.py:489
  147.8 0.5 collective-permute-done.9.from_right
  148.3 0.4 last.1
  148.7 0.7 slice.77
  (18 shorter events, 0.3 us)
Async XLA Ops:
  0.6 22.9 %collective-permute-start.3 = (f32[1,512]{1,0:T(1,128)}, f32[1,512]{1,0:T(1,128)S(1)}, u32[]{:S(2)}, u32[]{:S(2)}) collective-permute-start(f32[1,512]{1,0:T(1,128)} %bitcast.57), channel_id=1, source_target_pairs={{4,0},{8,4},{12,8},{16,12},{20,16},{24,20},{28,24},{0,28},{5,1},{9... | collective-permute-start | bytes 6152 | tf_op jit(solution)/shard_map/ppermute | solution.py:413
  6.7 16.9 %collective-permute-start.2 = (f32[1,512]{1,0:T(1,128)}, f32[1,512]{1,0:T(1,128)S(1)}, u32[]{:S(2)}, u32[]{:S(2)}) collective-permute-start(f32[1,512]{1,0:T(1,128)} %bitcast.58), channel_id=1, source_target_pairs={{0,4},{4,8},{8,12},{12,16},{16,20},{20,24},{24,28},{28,0},{1,5},{5... | collective-permute-start | bytes 6152 | tf_op jit(solution)/shard_map/ppermute | solution.py:412
  8.8 15.5 %all-to-all-start = ((f32[4,1,2048]{2,1,0:T(1,128)}), f32[4,1,2048]{2,1,0:T(1,128)S(1)}, u32[]{:S(2)}, u32[]{:S(2)}) async-start(f32[4,1,2048]{2,1,0:T(1,128)} %reshape.239), calls=%async_computation | async-start | bytes 65536 | tf_op jit(solution)/shard_map/all_to_all | solution.py:379
  13.9 62.7 %collective-permute-start = (f32[6,4,512]{2,1,0:T(4,128)S(1)}, f32[6,4,512]{2,1,0:T(4,128)S(1)}, u32[]{:S(2)}, u32[]{:S(2)}) collective-permute-start(f32[6,4,512]{2,1,0:T(4,128)S(1)} %get-tuple-element.35), channel_id=1, source_target_pairs={{0,1},{1,2},{2,3},{4,5},{5,6},{6,7},{8,9},{9,10},{10,11},{12,13},{... | collective-permute-start | bytes 147464 | tf_op jit(solution)/shard_map/ppermute | solution.py:393
  16.3 60.3 %collective-permute-start.1 = (f32[6,4,512]{2,1,0:T(4,128)S(1)}, f32[6,4,512]{2,1,0:T(4,128)S(1)}, u32[]{:S(2)}, u32[]{:S(2)}) collective-permute-start(f32[6,4,512]{2,1,0:T(4,128)S(1)} %get-tuple-element.36), channel_id=1, source_target_pairs={{1,0},{2,1},{3,2},{5,4},{6,5},{7,6},{9,8},{10,9},{11,10},{13,12},{... | collective-permute-start | bytes 147464 | tf_op jit(solution)/shard_map/ppermute | solution.py:395
  26.1 2.2 %copy-start.1 = (f32[32,8,4096]{2,1,0:T(8,128)S(1)}, f32[32,8,4096]{2,1,0:T(8,128)}, u32[]{:S(2)}) copy-start(f32[32,8,4096]{2,1,0:T(8,128)} %param.10) | copy-start | bytes 12582916
  70.5 11.3 %copy-start = (bf16[256,256]{1,0:T(8,128)(2,1)S(1)}, bf16[256,256]{1,0:T(8,128)(2,1)}, u32[]{:S(2)}) copy-start(bf16[256,256]{1,0:T(8,128)(2,1)} %constant.160.clone.derive) | copy-start | bytes 393220
  71.4 9.2 %all-to-all-start.1 = ((f32[4,1,3072]{2,1,0:T(1,128)}), f32[4,1,3072]{2,1,0:T(1,128)S(1)}, u32[]{:S(2)}, u32[]{:S(2)}) async-start(f32[4,1,3072]{2,1,0:T(1,128)} %reshape.241), calls=%async_computation.1 | async-start | bytes 98304 | tf_op jit(solution)/shard_map/all_to_all | solution.py:454
  82.4 6.8 %collective-permute-start.4 = (f32[96,128]{1,0:T(8,128)S(1)}, f32[96,128]{1,0:T(8,128)S(1)}, u32[]{:S(2)}, u32[]{:S(2)}) collective-permute-start(f32[96,128]{1,0:T(8,128)S(1)} %get-tuple-element.20), channel_id=1, source_target_pairs={{0,4},{4,8},{8,12},{12,16},{16,20},{20,24},{24,28},{28,0},{1,5},{5... | collective-permute-start | bytes 147464 | tf_op jit(solution)/shard_map/ppermute | solution.py:480
  82.5 6.8 %collective-permute-start.5 = (f32[96,128]{1,0:T(8,128)S(1)}, f32[96,128]{1,0:T(8,128)S(1)}, u32[]{:S(2)}, u32[]{:S(2)}) collective-permute-start(f32[96,128]{1,0:T(8,128)S(1)} %get-tuple-element.21), channel_id=1, source_target_pairs={{4,0},{8,4},{12,8},{16,12},{20,16},{24,20},{28,24},{0,28},{5,1},{9... | collective-permute-start | bytes 147464 | tf_op jit(solution)/shard_map/ppermute | solution.py:481
  90.3 47.6 %collective-permute-start.6 = (f32[96,128]{1,0:T(8,128)S(1)}, f32[96,128]{1,0:T(8,128)S(1)}, u32[]{:S(2)}, u32[]{:S(2)}) collective-permute-start(f32[96,128]{1,0:T(8,128)S(1)} %get-tuple-element.27), channel_id=1, source_target_pairs={{0,4},{4,8},{8,12},{12,16},{16,20},{20,24},{24,28},{28,0},{1,5},{5... | collective-permute-start | bytes 147464 | tf_op jit(solution)/shard_map/ppermute | solution.py:480
  135.8 4.1 %collective-permute-start.7 = (f32[96,128]{1,0:T(8,128)S(1)}, f32[96,128]{1,0:T(8,128)S(1)}, u32[]{:S(2)}, u32[]{:S(2)}) collective-permute-start(f32[96,128]{1,0:T(8,128)S(1)} %get-tuple-element.28), channel_id=1, source_target_pairs={{4,0},{8,4},{12,8},{16,12},{20,16},{24,20},{28,24},{0,28},{5,1},{9... | collective-permute-start | bytes 147464 | tf_op jit(solution)/shard_map/ppermute | solution.py:481
  140.9 6.9 %collective-permute-start.8 = (f32[96,128]{1,0:T(8,128)S(1)}, f32[96,128]{1,0:T(8,128)S(1)}, u32[]{:S(2)}, u32[]{:S(2)}) collective-permute-start(f32[96,128]{1,0:T(8,128)S(1)} %get-tuple-element.30), channel_id=1, source_target_pairs={{0,4},{4,8},{8,12},{12,16},{16,20},{20,24},{24,28},{28,0},{1,5},{5... | collective-permute-start | bytes 147464 | tf_op jit(solution)/shard_map/ppermute | solution.py:489
  143.9 4.4 %collective-permute-start.9 = (f32[96,128]{1,0:T(8,128)S(1)}, f32[96,128]{1,0:T(8,128)S(1)}, u32[]{:S(2)}, u32[]{:S(2)}) collective-permute-start(f32[96,128]{1,0:T(8,128)S(1)} %get-tuple-element.31), channel_id=1, source_target_pairs={{4,0},{8,4},{12,8},{16,12},{20,16},{24,20},{28,24},{0,28},{5,1},{9... | collective-permute-start | bytes 147464 | tf_op jit(solution)/shard_map/ppermute | solution.py:490
